TPU v7x, 32 devices: a whole 2x2x4 slice. The times are simulated.
32 devices in a mesh: energy: 8 (over z, y), momentum: 4 (over x, core).
Axes of the slice: x: 2, y: 2, z: 4, core: 2. Of those that a mesh axis runs over, the one named last changes fastest.
Arguments:
- device_hamiltonian: float32 [4, 2, 256, 256], P('momentum'), may hold values from -3 to 1, as said below
- lead_hamiltonian: float32 [4, 2, 256, 256], P('momentum'), may hold values from -3 to 1, as said below
- lead_coupling: float32 [4, 2, 256, 256], P('momentum'), may hold values from -0.28 to 0.28
- pair_atoms: int32 [2, 128], replicated, may hold values from 0 to 20, as said below
- phonon_shift: int32 [4], replicated, may hold values from 1 to 7
- occupation: float32 [4], replicated, may hold values from 0.2 to 1.5
- phonon_coupling: float32 [4, 128], replicated, may hold values from 0.1 to 0.4
Outputs:
- green_final: float32 [8, 4, 2, 256, 256], P('energy', 'momentum')
Inputs may be any that keep to these rules, and one draw needn't show every extreme that they name: `device_hamiltonian`: each diagonal entry has its real part in [-1, 1] and its imaginary part in [-3, -1.5]; off-diagonal entries lie within 0.21 in magnitude. `lead_hamiltonian`: each diagonal entry has its real part in [-1, 1] and its imaginary part in [-3, -1.5]; off-diagonal entries lie within 0.12 in magnitude. `pair_atoms`: the first 21 pairs join each atom with itself, in order; every other pair joins two different atoms.
All inputs are finite; a program needn't handle non-finite values.
Results may differ from a plain program's by a relative error of at most 0.00011.
Values sent between devices are 32-bit elements; how exact they have to be, the bound alone decides.
A program may use at most 64 MiB of HBM per device.

v0:
```python
import functools

import jax
import jax.numpy as jnp
from jax import lax
from jax.experimental import pallas as pl
from jax.experimental.pallas import tpu as pltpu
from jax.sharding import PartitionSpec as P

ORB = 12
NEWTON = 2
LANES = 128
F32 = jnp.float32
BF16 = jnp.bfloat16
MESH = pl.DeviceIdType.MESH
VMEM_SPEC = pl.BlockSpec(memory_space=pltpu.VMEM)
SMEM_SPEC = pl.BlockSpec(memory_space=pltpu.SMEM)


def split(value):
    high = value.astype(BF16)
    return high, (value - high.astype(F32)).astype(BF16)


def prepare(matrix):
    real, imag = matrix
    return split(real), split(imag), split(real + imag)


def real_product(left, right, transposed):
    dims = (((1,), (1 if transposed else 0,)), ((), ()))
    dot = functools.partial(lax.dot_general, dimension_numbers=dims, preferred_element_type=F32)
    return dot(left[0], right[0]) + (dot(left[0], right[1]) + dot(left[1], right[0]))


def complex_product(left, right, transposed=False):
    reals = real_product(left[0], right[0], transposed)
    imags = real_product(left[1], right[1], transposed)
    mixed = real_product(left[2], right[2], transposed)
    return reals - imags, mixed - reals - imags


def identity_mask(size):
    rows = lax.broadcasted_iota(jnp.int32, (size, size), 0)
    return rows == lax.broadcasted_iota(jnp.int32, (size, size), 1)


def inverse(real, imag):
    modulus = real * real + imag * imag
    return real / modulus, -imag / modulus


def diagonal_step(system, bare):
    eye = identity_mask(system[0].shape[0])
    masked = [jnp.where(eye, part, 0.0) for part in bare]
    row_real, row_imag = inverse(*[jnp.sum(part, axis=0, keepdims=True) for part in masked])
    col_real, col_imag = inverse(*[jnp.sum(part, axis=1, keepdims=True) for part in masked])
    step_real = system[0] * row_real - system[1] * row_imag
    step_imag = system[0] * row_imag + system[1] * row_real
    both_real = col_real * step_real - col_imag * step_imag
    both_imag = col_real * step_imag + col_imag * step_real
    return (
        jnp.where(eye, 2.0 * row_real, 0.0) - both_real,
        jnp.where(eye, 2.0 * row_imag, 0.0) - both_imag,
    )


def newton(system, current):
    factor = prepare(system)
    for _ in range(NEWTON):
        held = prepare(current)
        residual = complex_product(factor, held)
        change = complex_product(held, prepare(residual))
        current = (2.0 * current[0] - change[0], 2.0 * current[1] - change[1])
    return current


def column_choice(pairs_ref, first, size):
    columns = lax.broadcasted_iota(jnp.int32, (size, pairs_ref.shape[1]), 0)
    starts = ORB * pairs_ref[1:2, :]
    picks = [(columns == starts + (first + j)).astype(F32).astype(BF16) for j in range(2)]
    return jnp.concatenate(picks, axis=1)


def row_choice(pairs_ref, atoms_padded):
    atoms = lax.broadcasted_iota(jnp.int32, (atoms_padded, pairs_ref.shape[1]), 0)
    mask = (atoms == pairs_ref[0:1, :]).astype(F32)
    return jnp.concatenate([mask, mask], axis=1)


def first_kernel(energies, dh_ref, lh_ref, lc_ref, pairs_ref, system_ref, green_ref, blocks_ref, tall):
    size = dh_ref.shape[-1]
    pairs = pairs_ref.shape[1]
    energy = -1.0 + 2.0 * (lax.axis_index("energy").astype(F32) + 0.5) / energies
    eye = identity_mask(size)
    shift = jnp.where(eye, energy, 0.0)
    lead = (shift - lh_ref[0, 0], -lh_ref[0, 1])
    green_lead = newton(lead, diagonal_step(lead, lead))
    coupling = prepare((lc_ref[0, 0], lc_ref[0, 1]))
    contact = complex_product(
        prepare(complex_product(coupling, prepare(green_lead))), coupling, transposed=True
    )
    bare = (shift - dh_ref[0, 0], -dh_ref[0, 1])
    system = (bare[0] - contact[0], bare[1] - contact[1])
    system_ref[0] = system[0]
    system_ref[1] = system[1]
    green = newton(system, diagonal_step(system, bare))
    green_ref[0] = green[0]
    green_ref[1] = green[1]
    padded = tall.shape[2] // ORB
    for part in range(2):
        for lane in range(size // LANES):
            tall[part, lane, 0:size, :] = green[part][:, lane * LANES : (lane + 1) * LANES]
            tall[part, lane, size:, :] = jnp.zeros((padded * ORB - size, LANES), F32)
    rows = jnp.concatenate(
        [
            jnp.concatenate(
                [tall[part, lane, pl.ds(i, padded, stride=ORB), :] for lane in range(size // LANES)], axis=1
            )
            for part in range(2)
            for i in range(ORB)
        ],
        axis=0,
    )
    high, low = split(rows)
    mask = row_choice(pairs_ref, padded)
    for first in range(0, ORB, 2):
        choice = column_choice(pairs_ref, first, size)
        chosen = jnp.dot(high, choice, preferred_element_type=F32) + jnp.dot(
            low, choice, preferred_element_type=F32
        )
        total = jnp.sum(chosen.reshape(2 * ORB, padded, 2 * pairs) * mask[None], axis=1)
        for j in range(2):
            start = (first + j) * 2 * ORB
            blocks_ref[start : start + 2 * ORB, :] = total[:, j * pairs : (j + 1) * pairs]


def exchange_kernel(
    energies, momenta, shift_ref, occupation_ref, coupling_ref, blocks_ref, out_ref,
    weights, gathered, result, send_sem, recv_sem,
):
    devices = energies * momenta
    my_energy = lax.axis_index("energy")
    my_momentum = lax.axis_index("momentum")
    me = my_energy * momenta + my_momentum
    barrier = pltpu.get_barrier_semaphore()

    def peer(step):
        other = lax.rem(me + step, devices)
        return other, (other // momenta, lax.rem(other, momenta))

    def greet(step, carry):
        pl.semaphore_signal(barrier, inc=1, device_id=peer(step)[1], device_id_type=MESH)
        return carry

    lax.fori_loop(1, devices, greet, 0)
    pl.semaphore_wait(barrier, devices - 1)

    def send_blocks(step, carry):
        other, where = peer(step)
        pltpu.make_async_remote_copy(
            src_ref=blocks_ref.at[other], dst_ref=gathered.at[me],
            send_sem=send_sem.at[0], recv_sem=recv_sem.at[0],
            device_id=where, device_id_type=MESH,
        ).start()
        return carry

    lax.fori_loop(1, devices, send_blocks, 0)
    gathered[me] = blocks_ref[me]
    source = lax.broadcasted_iota(jnp.int32, (energies, 1, coupling_ref.shape[-1]), 0)
    couplings = [coupling_ref[m : m + 1, :][None] for m in range(coupling_ref.shape[0])]

    def weigh(target, carry):
        total = jnp.zeros(source.shape, F32)
        for m, strength in enumerate(couplings):
            level = occupation_ref[m]
            below = jnp.where(source == target - shift_ref[m], level, 0.0)
            above = jnp.where(source == target + shift_ref[m], level + 1.0, 0.0)
            total = total + (below + above) * strength
        weights[target] = total / momenta
        return carry

    lax.fori_loop(0, energies, weigh, 0)

    def all_of(buffer, semaphore):
        part = buffer.at[pl.ds(0, devices - 1)]
        pltpu.make_async_copy(part, part, semaphore).wait()

    all_of(blocks_ref, send_sem.at[0])
    all_of(gathered, recv_sem.at[0])
    sums = []
    for e in range(energies):
        total = gathered[e * momenta]
        for k in range(1, momenta):
            total = total + gathered[e * momenta + k]
        sums.append(total)

    def convolve(target, carry):
        total = sums[0] * weights[target, 0:1]
        for e in range(1, energies):
            total = total + sums[e] * weights[target, e : e + 1]
        result[target] = total
        return carry

    lax.fori_loop(0, energies, convolve, 0)

    def send_result(step, carry):
        other, where = peer(step)
        pltpu.make_async_remote_copy(
            src_ref=result.at[other // momenta], dst_ref=out_ref.at[me],
            send_sem=send_sem.at[1], recv_sem=recv_sem.at[1],
            device_id=where, device_id_type=MESH,
        ).start()
        return carry

    lax.fori_loop(1, devices, send_result, 0)
    out_ref[me] = result[my_energy]
    all_of(blocks_ref, send_sem.at[1])
    all_of(out_ref, recv_sem.at[1])


def final_kernel(system_ref, green_ref, blocks_ref, pairs_ref, out_ref, tall):
    size = system_ref.shape[-1]
    pairs = pairs_ref.shape[1]
    padded = tall.shape[2] // ORB
    mask = row_choice(pairs_ref, padded)
    spread = jnp.zeros((2 * ORB * padded, size), F32)
    for first in range(0, ORB, 2):
        start = first * 2 * ORB
        values = jnp.concatenate(
            [blocks_ref[start + j * 2 * ORB : start + (j + 1) * 2 * ORB, :] for j in range(2)], axis=1
        )
        wide = (values[:, None, :] * mask[None]).reshape(2 * ORB * padded, 2 * pairs)
        high, low = split(wide)
        choice = column_choice(pairs_ref, first, size)
        dims = (((1,), (1,)), ((), ()))
        spread = spread + lax.dot_general(high, choice, dims, preferred_element_type=F32)
        spread = spread + lax.dot_general(low, choice, dims, preferred_element_type=F32)
    for part in range(2):
        for i in range(ORB):
            start = (part * ORB + i) * padded
            for lane in range(size // LANES):
                tall[part, lane, pl.ds(i, padded, stride=ORB), :] = spread[
                    start : start + padded, lane * LANES : (lane + 1) * LANES
                ]
    system = tuple(
        system_ref[part]
        - jnp.concatenate([tall[part, lane, 0:size, :] for lane in range(size // LANES)], axis=1)
        for part in range(2)
    )
    final = newton(system, (green_ref[0], green_ref[1]))
    out_ref[0, 0, 0] = final[0]
    out_ref[0, 0, 1] = final[1]


def per_device(
    device_hamiltonian, lead_hamiltonian, lead_coupling, pair_atoms, phonon_shift, occupation, phonon_coupling
):
    energies = lax.axis_size("energy")
    momenta = lax.axis_size("momentum")
    devices = energies * momenta
    size = device_hamiltonian.shape[-1]
    pairs = pair_atoms.shape[1]
    entries = 2 * ORB * ORB
    share = -(-entries // devices)
    padded = 8 * (-(-size // (8 * ORB)))
    tall = pltpu.VMEM((2, size // LANES, padded * ORB, LANES), F32)
    params = functools.partial(pltpu.CompilerParams, vmem_limit_bytes=56 * 2**20)
    matrix = jax.ShapeDtypeStruct((2, size, size), F32)
    system, green, blocks = pl.pallas_call(
        functools.partial(first_kernel, energies),
        out_shape=(matrix, matrix, jax.ShapeDtypeStruct((entries, pairs), F32)),
        in_specs=[VMEM_SPEC] * 4,
        out_specs=(VMEM_SPEC,) * 3,
        scratch_shapes=[tall],
        compiler_params=params(),
        name="first_round",
    )(device_hamiltonian, lead_hamiltonian, lead_coupling, pair_atoms)
    blocks = jnp.pad(blocks, ((0, share * devices - entries), (0, 0))).reshape(devices, share, 1, pairs)
    received = pl.pallas_call(
        functools.partial(exchange_kernel, energies, momenta),
        out_shape=jax.ShapeDtypeStruct(blocks.shape, F32),
        in_specs=[SMEM_SPEC, SMEM_SPEC, VMEM_SPEC, VMEM_SPEC],
        out_specs=VMEM_SPEC,
        scratch_shapes=[
            pltpu.VMEM((energies, energies, 1, pairs), F32),
            pltpu.VMEM(blocks.shape, F32),
            pltpu.VMEM((energies,) + blocks.shape[1:], F32),
            pltpu.SemaphoreType.DMA((2,)),
            pltpu.SemaphoreType.DMA((2,)),
        ],
        compiler_params=params(collective_id=0, has_side_effects=True),
        name="exchange",
    )(phonon_shift, occupation, phonon_coupling, blocks)
    received = received.reshape(devices * share, pairs)[:entries]
    return pl.pallas_call(
        final_kernel,
        out_shape=jax.ShapeDtypeStruct((1, 1, 2, size, size), F32),
        in_specs=[VMEM_SPEC] * 4,
        out_specs=VMEM_SPEC,
        scratch_shapes=[tall],
        compiler_params=params(),
        name="final_round",
    )(system, green, received, pair_atoms)


def solution(mesh):
    matrices = P("momentum", None, None, None)
    return jax.shard_map(
        per_device,
        mesh=mesh,
        in_specs=(matrices, matrices, matrices, P(), P(), P(), P()),
        out_specs=P("energy", "momentum", None, None, None),
        check_vma=False,
    )
```

profile of v0, /device:TPU:0, one launch (start us, length us, event | category | flops | bytes accessed | tf_op | source)
XLA Modules:
  0.0 33.8 jit_solution(11970328296625816671)
XLA Ops:
  0.0 8.0 %first_round.1 = (f32[2,256,256]{2,1,0:T(8,128)}, f32[2,256,256]{2,1,0:T(8,128)}, f32[288,128]{1,0:T(8,128)}) custom-call(f32[1,2,256,256]{3,2,1,0:T(8,128)} %dh_ref.1, f32[1,2,256,256]{3,2,1,0:T(8,128)} %lh_ref.1, f32[1,2,256,256]{3,2,1,0:T(8,128)} %lc_ref.1, s32[2,128]{1,0:T(2,128)} %pairs_ref.3), custom_call_target="tpu_custom_call" | custom-call | tf_op jit(solution)/shard_map/first_round/pallas_call | solution.py:270
  8.0 19.5 %exchange.1 = f32[32,9,1,128]{3,2,1,0:T(1,128)} custom-call(s32[4]{0:T(128)} %shift_ref.1, f32[4]{0:T(128)} %occupation_ref.1, f32[4,128]{1,0:T(4,128)} %coupling_ref.1, f32[32,9,1,128]{3,2,1,0:T(1,128)} %bitcast.3), custom_call_target="tpu_custom_call" | custom-call | tf_op jit(solution)/shard_map/exchange/pallas_call | solution.py:280
  27.5 6.3 %final_round.1 = f32[1,1,2,256,256]{4,3,2,1,0:T(8,128)} custom-call(f32[2,256,256]{2,1,0:T(8,128)} %get-tuple-element.8.system_ref, f32[2,256,256]{2,1,0:T(8,128)} %get-tuple-element.9.green_ref, f32[288,128]{1,0:T(8,128)} %bitcast.2, s32[2,128]{1,0:T(2,128)} %pairs_ref.3), custom_call_target="tpu_custom_call" | custom-call | tf_op jit(solution)/shard_map/final_round/pallas_call | solution.py:296
where the time goes:
time: 34 us; the launch traced here: 33.8 us
  Pallas kernels  33.8 us (99%)
    pallas_call x1, Pallas kernels, per_device(): pl.pallas_call(functools.partial(exchange_kernel, energies, momenta), out...  19.5 us
    pallas_call x1, Pallas kernels, per_device(): pl.pallas_call(functools.partial(first_kernel, energies), out_shape=(matr...  8.04 us
    pallas_call x1, Pallas kernels, per_device(): pl.pallas_call(final_kernel, out_shape=jax.ShapeDtypeStruct((1, 1, 2, siz...  6.26 us

commit v1 on v0

--- a/solution.py
+++ b/solution.py
@@ -135,38 +135,45 @@
             blocks_ref[start : start + 2 * ORB, :] = total[:, j * pairs : (j + 1) * pairs]
 
 
+def each(count, body):
+    if count <= 16:
+        for step in range(1, count):
+            body(step)
+    else:
+        lax.fori_loop(1, count, lambda step, carry: (body(step), carry)[1], 0)
+
+
 def exchange_kernel(
     energies, momenta, shift_ref, occupation_ref, coupling_ref, blocks_ref, out_ref,
-    weights, gathered, result, send_sem, recv_sem,
+    weights, partner_half, half, gathered, result, send_sem, recv_sem,
 ):
-    devices = energies * momenta
+    halves, groups = blocks_ref.shape[:2]
+    columns = momenta // halves
     my_energy = lax.axis_index("energy")
     my_momentum = lax.axis_index("momentum")
-    me = my_energy * momenta + my_momentum
+    my_column = my_momentum // halves
+    my_half = lax.rem(my_momentum, halves)
+    me = my_energy * columns + my_column
+    other_half = halves - 1 - my_half
+    partner = (my_energy, my_column * halves + other_half)
     barrier = pltpu.get_barrier_semaphore()
 
     def peer(step):
-        other = lax.rem(me + step, devices)
-        return other, (other // momenta, lax.rem(other, momenta))
-
-    def greet(step, carry):
-        pl.semaphore_signal(barrier, inc=1, device_id=peer(step)[1], device_id_type=MESH)
-        return carry
-
-    lax.fori_loop(1, devices, greet, 0)
-    pl.semaphore_wait(barrier, devices - 1)
-
-    def send_blocks(step, carry):
-        other, where = peer(step)
-        pltpu.make_async_remote_copy(
-            src_ref=blocks_ref.at[other], dst_ref=gathered.at[me],
-            send_sem=send_sem.at[0], recv_sem=recv_sem.at[0],
+        other = lax.rem(me + step, groups)
+        return other, (other // columns, lax.rem(other, columns) * halves + my_half)
+
+    def send(source, target, phase, where):
+        return pltpu.make_async_remote_copy(
+            src_ref=source, dst_ref=target, send_sem=send_sem.at[phase], recv_sem=recv_sem.at[phase],
             device_id=where, device_id_type=MESH,
-        ).start()
-        return carry
-
-    lax.fori_loop(1, devices, send_blocks, 0)
-    gathered[me] = blocks_ref[me]
+        )
+
+    def greet(where):
+        pl.semaphore_signal(barrier, inc=1, device_id=where, device_id_type=MESH)
+
+    if halves > 1:
+        greet(partner)
+    each(groups, lambda step: greet(peer(step)[1]))
     source = lax.broadcasted_iota(jnp.int32, (energies, 1, coupling_ref.shape[-1]), 0)
     couplings = [coupling_ref[m : m + 1, :][None] for m in range(coupling_ref.shape[0])]
 
@@ -181,42 +188,61 @@
         return carry
 
     lax.fori_loop(0, energies, weigh, 0)
+    pl.semaphore_wait(barrier, groups - 1 + halves - 1)
+
+    if halves > 1:
+        swap = send(blocks_ref.at[other_half], partner_half, 0, partner)
+        swap.start()
+        swap.wait()
+        half[...] = blocks_ref[my_half] + partner_half[...]
+    else:
+        half[...] = blocks_ref[0]
+
+    def send_blocks(step):
+        other, where = peer(step)
+        send(half.at[other], gathered.at[me], 1, where).start()
+
+    each(groups, send_blocks)
+    gathered[me] = half[me]
 
     def all_of(buffer, semaphore):
-        part = buffer.at[pl.ds(0, devices - 1)]
+        part = buffer.at[pl.ds(0, groups - 1)]
         pltpu.make_async_copy(part, part, semaphore).wait()
 
-    all_of(blocks_ref, send_sem.at[0])
-    all_of(gathered, recv_sem.at[0])
+    all_of(gathered, recv_sem.at[1])
     sums = []
     for e in range(energies):
-        total = gathered[e * momenta]
-        for k in range(1, momenta):
-            total = total + gathered[e * momenta + k]
+        total = gathered[e * columns]
+        for k in range(1, columns):
+            total = total + gathered[e * columns + k]
         sums.append(total)
 
-    def convolve(target, carry):
+    def convolve(target):
         total = sums[0] * weights[target, 0:1]
         for e in range(1, energies):
             total = total + sums[e] * weights[target, e : e + 1]
         result[target] = total
-        return carry
-
-    lax.fori_loop(0, energies, convolve, 0)
-
-    def send_result(step, carry):
-        other, where = peer(step)
-        pltpu.make_async_remote_copy(
-            src_ref=result.at[other // momenta], dst_ref=out_ref.at[me],
-            send_sem=send_sem.at[1], recv_sem=recv_sem.at[1],
-            device_id=where, device_id_type=MESH,
-        ).start()
-        return carry
-
-    lax.fori_loop(1, devices, send_result, 0)
-    out_ref[me] = result[my_energy]
-    all_of(blocks_ref, send_sem.at[1])
-    all_of(out_ref, recv_sem.at[1])
+
+    def send_result(step):
+        target = lax.rem(my_energy + step, energies)
+        convolve(target)
+        for k in range(columns):
+            where = (target, k * halves + my_half)
+            send(result.at[target], out_ref.at[my_half, me], 2, where).start()
+
+    each(energies, send_result)
+    convolve(my_energy)
+    for k in range(1, columns):
+        where = (my_energy, lax.rem(my_column + k, columns) * halves + my_half)
+        send(result.at[my_energy], out_ref.at[my_half, me], 2, where).start()
+    out_ref[my_half, me] = result[my_energy]
+    all_of(out_ref.at[0], recv_sem.at[2])
+    if halves > 1:
+        share = send(out_ref.at[my_half], out_ref.at[my_half], 3, partner)
+        share.start()
+        share.wait()
+    all_of(half, send_sem.at[1])
+    all_of(half, send_sem.at[2])
 
 
 def final_kernel(system_ref, green_ref, blocks_ref, pairs_ref, out_ref, tall):
@@ -258,11 +284,12 @@
 ):
     energies = lax.axis_size("energy")
     momenta = lax.axis_size("momentum")
-    devices = energies * momenta
+    halves = 2 if momenta % 2 == 0 else 1
+    groups = energies * momenta // halves
     size = device_hamiltonian.shape[-1]
     pairs = pair_atoms.shape[1]
     entries = 2 * ORB * ORB
-    share = -(-entries // devices)
+    share = -(-entries // (halves * groups))
     padded = 8 * (-(-size // (8 * ORB)))
     tall = pltpu.VMEM((2, size // LANES, padded * ORB, LANES), F32)
     params = functools.partial(pltpu.CompilerParams, vmem_limit_bytes=56 * 2**20)
@@ -276,7 +303,8 @@
         compiler_params=params(),
         name="first_round",
     )(device_hamiltonian, lead_hamiltonian, lead_coupling, pair_atoms)
-    blocks = jnp.pad(blocks, ((0, share * devices - entries), (0, 0))).reshape(devices, share, 1, pairs)
+    filled = halves * groups * share
+    blocks = jnp.pad(blocks, ((0, filled - entries), (0, 0))).reshape(halves, groups, share, 1, pairs)
     received = pl.pallas_call(
         functools.partial(exchange_kernel, energies, momenta),
         out_shape=jax.ShapeDtypeStruct(blocks.shape, F32),
@@ -284,15 +312,17 @@
         out_specs=VMEM_SPEC,
         scratch_shapes=[
             pltpu.VMEM((energies, energies, 1, pairs), F32),
-            pltpu.VMEM(blocks.shape, F32),
-            pltpu.VMEM((energies,) + blocks.shape[1:], F32),
-            pltpu.SemaphoreType.DMA((2,)),
-            pltpu.SemaphoreType.DMA((2,)),
+            pltpu.VMEM(blocks.shape[1:], F32),
+            pltpu.VMEM(blocks.shape[1:], F32),
+            pltpu.VMEM(blocks.shape[1:], F32),
+            pltpu.VMEM((energies,) + blocks.shape[2:], F32),
+            pltpu.SemaphoreType.DMA((4,)),
+            pltpu.SemaphoreType.DMA((4,)),
         ],
         compiler_params=params(collective_id=0, has_side_effects=True),
         name="exchange",
     )(phonon_shift, occupation, phonon_coupling, blocks)
-    received = received.reshape(devices * share, pairs)[:entries]
+    received = received.reshape(filled, pairs)[:entries]
     return pl.pallas_call(
         final_kernel,
         out_shape=jax.ShapeDtypeStruct((1, 1, 2, size, size), F32),

time: 34 us -> 34.7 us (1.021)
  Pallas kernels: 33.8 us -> 34.5 us
    pallas_call x1, Pallas kernels: 19.5 us -> 20.2 us  [per_device(): pl.pallas_call(functools.partial(exchange_kernel, energies, momenta), out...]
where the time goes in v1:
time: 34.7 us; the launch traced here: 34.5 us
  Pallas kernels  34.5 us (99%)
    pallas_call x1, Pallas kernels, per_device(): pl.pallas_call(functools.partial(exchange_kernel, energies, momenta), out...  20.2 us
    pallas_call x1, Pallas kernels, per_device(): pl.pallas_call(functools.partial(first_kernel, energies), out_shape=(matr...  8.04 us
    pallas_call x1, Pallas kernels, per_device(): pl.pallas_call(final_kernel, out_shape=jax.ShapeDtypeStruct((1, 1, 2, siz...  6.26 us

profile of v1, /device:TPU:0, one launch (start us, length us, event | category | flops | bytes accessed | tf_op | source)
XLA Modules:
  0.0 34.5 jit_solution(1886629996143145168)
XLA Ops:
  0.0 8.0 %first_round.1 = (f32[2,256,256]{2,1,0:T(8,128)}, f32[2,256,256]{2,1,0:T(8,128)}, f32[288,128]{1,0:T(8,128)}) custom-call(f32[1,2,256,256]{3,2,1,0:T(8,128)} %dh_ref.1, f32[1,2,256,256]{3,2,1,0:T(8,128)} %lh_ref.1, f32[1,2,256,256]{3,2,1,0:T(8,128)} %lc_ref.1, s32[2,128]{1,0:T(2,128)} %pairs_ref.3), custom_call_target="tpu_custom_call" | custom-call | tf_op jit(solution)/shard_map/first_round/pallas_call | solution.py:297
  8.0 20.2 %exchange.1 = f32[2,16,9,1,128]{4,3,2,1,0:T(1,128)} custom-call(s32[4]{0:T(128)} %shift_ref.1, f32[4]{0:T(128)} %occupation_ref.1, f32[4,128]{1,0:T(4,128)} %coupling_ref.1, f32[2,16,9,1,128]{4,3,2,1,0:T(1,128)} %bitcast.3), custom_call_target="tpu_custom_call" | custom-call | tf_op jit(solution)/shard_map/exchange/pallas_call | solution.py:308
  28.2 6.3 %final_round.1 = f32[1,1,2,256,256]{4,3,2,1,0:T(8,128)} custom-call(f32[2,256,256]{2,1,0:T(8,128)} %get-tuple-element.8.system_ref, f32[2,256,256]{2,1,0:T(8,128)} %get-tuple-element.9.green_ref, f32[288,128]{1,0:T(8,128)} %bitcast.2, s32[2,128]{1,0:T(2,128)} %pairs_ref.3), custom_call_target="tpu_custom_call" | custom-call | tf_op jit(solution)/shard_map/final_round/pallas_call | solution.py:326
